TPU v7x, 32 devices: a whole 2x2x4 slice. The times are simulated.
32 devices in a mesh: row: 4 (over y, core), col: 8 (over z, x).
Axes of the slice: x: 2, y: 2, z: 4, core: 2. Of those that a mesh axis runs over, the one named last changes fastest.
Arguments:
- a_values: float32 [256, 64, 448], P(('row', 'col')), may hold values from -0.75 to 0.75
- a_columns: int32 [256, 7], P(('row', 'col')), may hold values from 0 to 255, as said below
- p_values: float32 [256, 64, 256], P(('row', 'col')), may hold values from -0.75 to 0.75
- p_columns: int32 [256, 4], P(('row', 'col')), may hold values from 0 to 3
- p_count: int32 [256], P(('row', 'col')), may hold values from 1 to 4
- aggregates: int32 [256], P(('row', 'col')), may hold values from 0 to 3, as said below
Outputs:
- coarse_operator: float32 [128, 64, 1280], P(('row', 'col'))
Inputs may be any that keep to these rules, and one draw needn't show every extreme that they name: `a_columns`: slot 0 of each fine block row names that row itself; every slot names a fine block row of the row's own subdomain or of one of its neighbours 1 to 4; repeated columns add. Each of a subdomain's 4 aggregates holds at least one of its fine block rows.
All inputs are finite; a program needn't handle non-finite values.
Results may differ from a plain program's by a relative error of at most 0.0003.
Values sent between devices are 32-bit elements; how exact they have to be, the bound alone decides.
No kernel may reach another device: no remote copies, remote signals or barrier semaphores. Data moves between devices by JAX's collectives and lax.ppermute only.
A program may use at most 64 MiB of HBM per device.

v0:
```python
import functools

import jax
import jax.numpy as jnp
from jax import lax
from jax.experimental import pallas as pl
from jax.experimental.pallas import tpu as pltpu
from jax.sharding import PartitionSpec as P

CFG = {'parts': (3, 3, 2), 'xg': 0, 'la': None, 'tick': 1, 'ck': 100000000, 'gk': (2,), 'gf': (), 'rg': None, 'rs': 1, 'pr': 2, 'ch': 1, 'cl': 100000000000, 'ct': 1000000000, 'cp': 100000000, 'ca': 1000, 'cz': 1000, 'cut': 8, 'lb': None, 'g1': []}

BS = 64
KA = 7
KP = 4
CA = 4
WIDE = CA * BS
PARTS = CFG['parts']

OWN, PAIR_COL, FAR_COL, PAIR_ROW, FAR_ROW = range(5)

VMEM = pl.BlockSpec(memory_space=pltpu.VMEM)
HBM = pl.BlockSpec(memory_space=pltpu.HBM)
MIB = 1024 * 1024


def split(value):
    high = value.astype(jnp.bfloat16)
    low = (value - high.astype(jnp.float32)).astype(jnp.bfloat16)
    return high, low


def product(high, low, other):
    other_high, other_low = split(other)
    dot = functools.partial(jnp.dot, preferred_element_type=jnp.float32)
    return dot(high, other_high) + (dot(high, other_low) + dot(low, other_high))


def in_hbm(value):
    return pltpu.with_memory_space_constraint(value, pltpu.HBM)


def in_vmem(value):
    return pltpu.with_memory_space_constraint(value, pltpu.VMEM)


def cost(flops, moved):
    return pl.CostEstimate(flops=flops, bytes_accessed=moved, transcendentals=0)


def dense_row(row, values, columns, counts, aggregates):
    lane = lax.broadcasted_iota(jnp.int32, (1, 2 * BS), 1)
    lower = lane < BS
    diagonal = (
        lax.broadcasted_iota(jnp.int32, (BS, 2 * BS), 0)
        == lax.broadcasted_iota(jnp.int32, (BS, 2 * BS), 1) % BS
    ).astype(jnp.float32)
    live = counts[row]
    feeds = [jnp.where(k < live, columns[k, row], -1) for k in range(KP)]
    pieces = []
    for m in range(KP // 2):
        straight = values[:, m * 2 * BS : (m + 1) * 2 * BS]
        pieces.append((jnp.where(lower, feeds[2 * m], feeds[2 * m + 1]), straight))
        pieces.append(
            (jnp.where(lower, feeds[2 * m + 1], feeds[2 * m]), pltpu.roll(straight, BS, 1))
        )
    dense = []
    for j in range(CA // 2):
        wanted = jnp.where(lower, 2 * j, 2 * j + 1)
        total = jnp.where(wanted == aggregates[row], diagonal, 0.0)
        for feed, piece in pieces:
            total = total + jnp.where(feed == wanted, piece, 0.0)
        dense.append(total)
    return jnp.concatenate(dense, axis=1)


def dense_kernel(values_ref, columns_ref, counts_ref, aggregates_ref, *refs):
    count = len(PARTS)
    part_refs = refs[:count]
    dense_ref, values, columns, counts, aggregates, sems = refs[count:]
    small = [
        pltpu.make_async_copy(source, target, sems.at[index])
        for index, (source, target) in enumerate(
            [(columns_ref, columns), (counts_ref, counts), (aggregates_ref, aggregates)]
        )
    ]
    spans = [pl.ds(sum(PARTS[:part]), PARTS[part]) for part in range(count)]
    large = [
        pltpu.make_async_copy(values_ref.at[span], values.at[span], sems.at[3 + part])
        for part, span in enumerate(spans)
    ]
    for copy in small + large:
        copy.start()
    for copy in small:
        copy.wait()
    for part in range(count):
        large[part].wait()
        for index in range(PARTS[part]):
            row = sum(PARTS[:part]) + index
            dense = dense_row(row, values[row], columns, counts, aggregates)
            part_refs[part][index] = dense
            dense_ref[row] = dense


def dense_rows(p_values, p_columns, p_count, aggregates):
    every = p_values.shape[0]
    *parts, dense = pl.pallas_call(
        dense_kernel,
        in_specs=[HBM] * 4,
        out_specs=[VMEM] * (len(PARTS) + 1),
        out_shape=[pltpu.VMEM((rows, BS, WIDE), jnp.float32) for rows in (*PARTS, every)],
        scratch_shapes=[
            pltpu.VMEM(p_values.shape, jnp.float32),
            pltpu.SMEM((KP, every), jnp.int32),
            pltpu.SMEM((every,), jnp.int32),
            pltpu.SMEM((every,), jnp.int32),
            pltpu.SemaphoreType.DMA((3 + len(PARTS),)),
        ],
        cost_estimate=cost(400000, p_values.size * 12),
        name="dense_rows",
    )(in_hbm(p_values), in_hbm(p_columns.T), in_hbm(p_count), in_hbm(aggregates))
    return parts, dense


def put_block(group, block_ref, out_ref, sem):
    at = pl.multiple_of(group * WIDE, WIDE)
    copy = pltpu.make_async_copy(block_ref, out_ref.at[:, :, pl.ds(at, WIDE)], sem)
    copy.start()
    return copy


def left_kernel(col_count, first, dense_ref, columns_ref, a_ref, *refs):
    left, a, columns, sems = refs[-4:]
    rows = dense_ref.shape[0]
    mine = a.shape[0]
    grid_row = lax.axis_index("row")
    grid_col = lax.axis_index("col")
    small = pltpu.make_async_copy(columns_ref, columns, sems.at[0])
    small.start()
    large = [pltpu.make_async_copy(a_ref.at[first + row], a.at[row], sems.at[1 + row]) for row in range(mine)]
    for copy in large:
        copy.start()
    if first == 0:
        left[...] = jnp.zeros_like(left)
    for copy in large:
        copy.wait()
    small.wait()
    for index in range(mine):
        row = first + index
        a_high, a_low = split(a[index])
        p_high, p_low = split(dense_ref[row])
        turned_a = jnp.concatenate([a_high, a_low], axis=0).T
        term = jnp.dot(
            jnp.concatenate([turned_a, turned_a], axis=1),
            jnp.concatenate([p_high, p_high, p_low, p_low], axis=0),
            preferred_element_type=jnp.float32,
        )
        for slot in range(KA):
            target = columns[row, slot]
            sub = target // rows
            sub_row = sub // col_count
            sub_col = sub - sub_row * col_count
            along = jnp.where(sub_col == grid_col, OWN, jnp.where(sub_col == (grid_col ^ 1), PAIR_COL, FAR_COL))
            across = jnp.where(sub_row == (grid_row ^ 1), PAIR_ROW, FAR_ROW)
            group = jnp.where(sub_row == grid_row, along, across)
            at = pl.multiple_of((group * rows + (target - sub * rows)) * BS, BS)
            left[pl.ds(at, BS), :] += term[slot * BS : (slot + 1) * BS]


def left_product(dense, a_columns, a_values, before, first, count, col_count):
    rows = a_values.shape[0]
    given = [] if before is None else [before]
    return pl.pallas_call(
        functools.partial(left_kernel, col_count, first),
        in_specs=[VMEM, HBM, HBM] + [VMEM] * len(given),
        out_specs=VMEM,
        out_shape=pltpu.VMEM((5 * rows * BS, WIDE), jnp.float32),
        scratch_shapes=[
            pltpu.VMEM((count, *a_values.shape[1:]), jnp.float32),
            pltpu.SMEM(a_columns.shape, jnp.int32),
            pltpu.SemaphoreType.DMA((1 + count,)),
        ],
        input_output_aliases={3: 0} if given else {},
        compiler_params=pltpu.CompilerParams(vmem_limit_bytes=16 * MIB),
        cost_estimate=cost(CFG['cl'], 4000),
        name="left_product",
    )(in_vmem(dense), in_hbm(a_columns), in_hbm(a_values), *map(in_vmem, given))


def turn_kernel(left_ref, high_ref, low_ref):
    depth = high_ref.shape[2]
    for place in range(5):
        high_ref[place], low_ref[place] = split(left_ref[place * depth : (place + 1) * depth, :].T)


def turned(left):
    depth = left.shape[0] // 5
    return pl.pallas_call(
        turn_kernel,
        in_specs=[VMEM],
        out_specs=[VMEM, VMEM],
        out_shape=[pltpu.VMEM((5, WIDE, depth), jnp.bfloat16)] * 2,
        compiler_params=pltpu.CompilerParams(vmem_limit_bytes=16 * MIB),
        cost_estimate=cost(CFG['ct'], 5000),
        name="turned",
    )(in_vmem(left))


def groups_here():
    col_odd = lax.axis_index("col") % 2
    row_odd = lax.axis_index("row") % 2
    return {OWN: 0, PAIR_COL: 2 - col_odd, FAR_COL: 1 + col_odd, PAIR_ROW: 4 - row_odd, FAR_ROW: 3 + row_odd}


def summed(high_ref, low_ref, place, part_refs, at=0):
    total = None
    for part_ref in part_refs:
        depth = part_ref.shape[0] * BS
        term = product(
            high_ref[place, :, at : at + depth], low_ref[place, :, at : at + depth], part_ref[...].reshape(depth, WIDE)
        )
        total = term if total is None else total + term
        at += depth
    return total.reshape(CA, BS, WIDE)


def products_kernel(places, counts, given, *refs):
    high_ref, low_ref, *refs = refs[given:]
    part_refs = refs[: sum(counts)]
    out_ref, blocks, sems = refs[sum(counts) :]
    groups = groups_here()
    copies = []
    for index, place in enumerate(places):
        at = sum(counts[:index])
        blocks[index] = summed(high_ref, low_ref, place, part_refs[at : at + counts[index]])
        copies.append(put_block(groups[place], blocks.at[index], out_ref, sems.at[index]))
    for copy in copies:
        copy.wait()


def products(out, high, low, parts):
    places = tuple(parts)
    counts = tuple(len(parts[place]) for place in places)
    flat = [part for place in places for part in parts[place]]
    given = [] if out is None else [out]
    return pl.pallas_call(
        functools.partial(products_kernel, places, counts, len(given)),
        in_specs=[HBM] * len(given) + [VMEM] * (2 + len(flat)),
        out_specs=HBM,
        out_shape=jax.ShapeDtypeStruct((CA, BS, 5 * WIDE), jnp.float32),
        scratch_shapes=[
            pltpu.VMEM((len(places), CA, BS, WIDE), jnp.float32),
            pltpu.SemaphoreType.DMA((len(places),)),
        ],
        input_output_aliases={0: 0} if given else {},
        compiler_params=pltpu.CompilerParams(vmem_limit_bytes=16 * MIB),
        cost_estimate=cost(CFG['cp'] * len(places), 2000),
        name="products",
    )(*given, *map(in_vmem, (high, low, *flat)))


def partial_kernel(place, at, chained, high_ref, low_ref, *refs):
    part_refs = refs[:-1]
    if chained:
        before_ref, *part_refs = part_refs
        refs[-1][...] = before_ref[...] + summed(high_ref, low_ref, place, part_refs, at)
    else:
        refs[-1][...] = summed(high_ref, low_ref, place, part_refs, at)


def partial_product(high, low, before, parts, place, at):
    given = [] if before is None else [before]
    return pl.pallas_call(
        functools.partial(partial_kernel, place, at, bool(given)),
        in_specs=[VMEM] * (2 + len(given) + len(parts)),
        out_specs=VMEM,
        out_shape=pltpu.VMEM((CA, BS, WIDE), jnp.float32),
        compiler_params=pltpu.CompilerParams(vmem_limit_bytes=16 * MIB),
        cost_estimate=cost(CFG['ca'], 1500),
        name="partial_product",
    )(*map(in_vmem, (high, low, *given, *parts)))


def last_kernel(place, at, out_in_ref, high_ref, low_ref, before_ref, part_ref, out_ref, block, sem):
    del out_in_ref
    block[...] = before_ref[...] + summed(high_ref, low_ref, place, [part_ref], at)
    put_block(groups_here()[place], block, out_ref, sem).wait()


def last_product(out, high, low, before, part, place, at):
    return pl.pallas_call(
        functools.partial(last_kernel, place, at),
        in_specs=[HBM] + [VMEM] * 4,
        out_specs=HBM,
        out_shape=jax.ShapeDtypeStruct(out.shape, out.dtype),
        scratch_shapes=[pltpu.VMEM((CA, BS, WIDE), jnp.float32), pltpu.SemaphoreType.DMA],
        input_output_aliases={0: 0},
        compiler_params=pltpu.CompilerParams(vmem_limit_bytes=16 * MIB),
        cost_estimate=cost(CFG['cz'], 700),
        name="last_product",
    )(out, *map(in_vmem, (high, low, before, part)))


def column_pairs(count):
    return [(i, i ^ 1) for i in range(count)]


def column_onward(count):
    return [(i, ((i ^ 1) + 1) % count if (i ^ 1) % 2 else ((i ^ 1) - 1) % count) for i in range(count)]


def row_pairs(count):
    return [(i, i ^ 1) for i in range(count)]


def row_between(count):
    pairs = [(i, i + 1) for i in range(1, count - 1, 2)]
    return pairs + [(b, a) for a, b in pairs]


def after(value, *others):
    return lax.optimization_barrier((value, *others))[0]


def tick_kernel(value_ref, out_ref):
    out_ref[...] = value_ref[0, :8, :128]


def tick(value, flops):
    return pl.pallas_call(
        tick_kernel,
        in_specs=[VMEM],
        out_specs=VMEM,
        out_shape=pltpu.VMEM((8, 128), jnp.float32),
        cost_estimate=cost(flops, 2000),
        name="tick",
    )(in_vmem(value))


def per_device(a_values, a_columns, p_values, p_columns, p_count, aggregates):
    row_count = lax.axis_size("row")
    col_count = lax.axis_size("col")
    depth = a_values.shape[0] * BS
    pairs, onward = column_pairs(col_count), column_onward(col_count)
    parts, dense = dense_rows(p_values, p_columns, p_count, aggregates)
    pair, far = [], []
    for index, part in enumerate(parts):
        if CFG['xg'] and index >= CFG['xg']:
            part = after(part, pair[index - CFG['xg']])
        pair.append(lax.ppermute(part, "col", pairs))
    own = dense
    if CFG['la'] is not None:
        own = after(dense, pair[CFG['la']])
    cut = CFG['cut']
    rows = a_values.shape[0]
    left = first = left_product(own, a_columns, a_values, None, 0, cut, col_count)
    if cut < rows:
        again = dense if CFG['lb'] is None else after(dense, pair[min(CFG['lb'], len(pair) - 1)])
        left = left_product(again, a_columns, a_values, first, cut, rows - cut, col_count)
    ticked = tick(parts[0], CFG['ck']) if CFG['tick'] else None
    for index, part in enumerate(pair):
        if index in CFG['gf']:
            part = after(part, left)
        if index in CFG['g1']:
            part = after(part, first)
        if CFG['tick'] and index in CFG['gk']:
            part = after(part, ticked)
        far.append(lax.ppermute(part, "col", onward))
    to_row = dense
    if CFG['rg'] == 'left':
        to_row = after(dense, left)
    elif CFG['rg'] == 'tick' and CFG['tick']:
        to_row = after(dense, ticked)
    elif isinstance(CFG['rg'], int):
        to_row = after(dense, pair[CFG['rg']])
    if CFG['rs']:
        pair_row = lax.ppermute(to_row, "row", row_pairs(row_count))
        far_row = lax.ppermute(to_row, "row", row_between(row_count))
    else:
        far_row = lax.ppermute(to_row, "row", row_between(row_count))
        pair_row = lax.ppermute(to_row, "row", row_pairs(row_count))
    high, low = turned(left)
    if CFG['pr'] == 0:
        out = products(None, high, low, {OWN: [dense], PAIR_ROW: [pair_row], FAR_ROW: [far_row], PAIR_COL: pair})
    elif CFG['pr'] == 1:
        out = products(None, high, low, {OWN: [dense], PAIR_ROW: [pair_row], FAR_ROW: [far_row]})
        out = products(out, high, low, {PAIR_COL: pair})
    elif CFG['pr'] == 2:
        out = products(None, high, low, {OWN: [dense], PAIR_COL: pair})
        out = products(out, high, low, {PAIR_ROW: [pair_row], FAR_ROW: [far_row]})
    if CFG['ch']:
        before, at = None, 0
        for part in far[:-1]:
            before = partial_product(high, low, before, [part], FAR_COL, at)
            at += part.shape[0] * BS
    else:
        before = partial_product(high, low, None, far[:-1], FAR_COL, 0)
    return last_product(out, high, low, before, far[-1], FAR_COL, depth - PARTS[-1] * BS)


def solution(mesh):
    in_specs = (
        P(("row", "col"), None, None),
        P(("row", "col"), None),
        P(("row", "col"), None, None),
        P(("row", "col"), None),
        P(("row", "col")),
        P(("row", "col")),
    )
    out_specs = P(("row", "col"), None, None)
    return jax.shard_map(
        per_device, mesh=mesh, in_specs=in_specs, out_specs=out_specs, check_vma=False
    )
```

profile of v0, /device:TPU:0, one launch (start us, length us, event | category | flops | bytes accessed | tf_op | source)
XLA Modules:
  0.0 26.7 jit_solution(12469137934180810407)
XLA Ops:
  0.0 1.3 %dense_rows.1 = (f32[3,64,256]{2,1,0:T(8,128)S(1)}, f32[3,64,256]{2,1,0:T(8,128)S(1)}, f32[2,64,256]{2,1,0:T(8,128)S(1)}, f32[8,64,256]{2,1,0:T(8,128)S(1)}) custom-call(f32[8,64,256]{2,1,0:T(8,128)} %values_ref.1, s32[4,8]{1,0:T(4,128)} %bitcast.1, s32[8]{0:T(128)} %counts_ref.1, s32[8]{0:T(128)} %aggregates_ref.1), custom_call_target="tpu_custom_call" | custom-call | flops 400000 | bytes 1572864 | tf_op jit(solution)/shard_map/dense_rows/pallas_call | solution.py:106
  1.3 3.0 %collective-permute-start = (f32[3,64,256]{2,1,0:T(8,128)S(1)}, f32[3,64,256]{2,1,0:T(8,128)S(1)}, u32[]{:S(2)}, u32[]{:S(2)}) collective-permute-start(f32[3,64,256]{2,1,0:T(8,128)S(1)} %get-tuple-element.14), channel_id=1, source_target_pairs={{0,1},{1,0},{2,3},{3,2},{4,5},{5,4},{6,7},{7,6},{8,9},{9,8},{10,11... | collective-permute-start | bytes 589832 | tf_op jit(solution)/shard_map/ppermute | solution.py:349
  4.3 0.1 collective-permute-start.1
  4.4 0.0 collective-permute-start.3
  4.4 0.7 %collective-permute-start.4 = (f32[8,64,256]{2,1,0:T(8,128)S(1)}, f32[8,64,256]{2,1,0:T(8,128)S(1)}, u32[]{:S(2)}, u32[]{:S(2)}) collective-permute-start(f32[8,64,256]{2,1,0:T(8,128)S(1)} %get-tuple-element.11.dense_ref.refs_2_), channel_id=1, source_target_pairs={{8,16},{16,8},{9,17},{17,9},{10,18},{18,10},{11,19},{19,11},{12,20... | collective-permute-start | bytes 1572872 | tf_op jit(solution)/shard_map/ppermute | solution.py:377
  5.1 2.0 %collective-permute-start.2 = (f32[2,64,256]{2,1,0:T(8,128)S(1)}, f32[2,64,256]{2,1,0:T(8,128)S(1)}, u32[]{:S(2)}, u32[]{:S(2)}) collective-permute-start(f32[2,64,256]{2,1,0:T(8,128)S(1)} %get-tuple-element.16), channel_id=1, source_target_pairs={{0,1},{1,0},{2,3},{3,2},{4,5},{5,4},{6,7},{7,6},{8,9},{9,8},{10,11... | collective-permute-start | bytes 393224 | tf_op jit(solution)/shard_map/ppermute | solution.py:349
  7.1 2.9 %collective-permute-done.refs_3_ = f32[3,64,256]{2,1,0:T(8,128)S(1)} collective-permute-done((f32[3,64,256]{2,1,0:T(8,128)S(1)}, f32[3,64,256]{2,1,0:T(8,128)S(1)}, u32[]{:S(2)}, u32[]{:S(2)}) %collective-permute-start) | collective-permute-done | bytes 196640 | tf_op jit(solution)/shard_map/ppermute | solution.py:349
  10.1 2.1 %collective-permute-start.5 = (f32[3,64,256]{2,1,0:T(8,128)S(1)}, f32[3,64,256]{2,1,0:T(8,128)S(1)}, u32[]{:S(2)}, u32[]{:S(2)}) collective-permute-start(f32[3,64,256]{2,1,0:T(8,128)S(1)} %collective-permute-done.refs_3_), channel_id=1, source_target_pairs={{0,2},{1,7},{2,4},{3,1},{4,6},{5,3},{6,0},{7,5},{8,10},{9,15},{10,... | collective-permute-start | bytes 589832 | tf_op jit(solution)/shard_map/ppermute | solution.py:367
  12.2 2.1 %collective-permute-done.1.refs_4_ = f32[3,64,256]{2,1,0:T(8,128)S(1)} collective-permute-done((f32[3,64,256]{2,1,0:T(8,128)S(1)}, f32[3,64,256]{2,1,0:T(8,128)S(1)}, u32[]{:S(2)}, u32[]{:S(2)}) %collective-permute-start.1) | collective-permute-done | bytes 196640 | tf_op jit(solution)/shard_map/ppermute | solution.py:349
  14.3 2.1 %collective-permute-start.6 = (f32[3,64,256]{2,1,0:T(8,128)S(1)}, f32[3,64,256]{2,1,0:T(8,128)S(1)}, u32[]{:S(2)}, u32[]{:S(2)}) collective-permute-start(f32[3,64,256]{2,1,0:T(8,128)S(1)} %collective-permute-done.1.refs_4_), channel_id=1, source_target_pairs={{0,2},{1,7},{2,4},{3,1},{4,6},{5,3},{6,0},{7,5},{8,10},{9,15},{10,... | collective-permute-start | bytes 589832 | tf_op jit(solution)/shard_map/ppermute | solution.py:367
  16.4 2.4 %left_product.1.left_ref = f32[2560,256]{1,0:T(8,128)S(1)} custom-call(f32[8,64,256]{2,1,0:T(8,128)S(1)} %get-tuple-element.11.dense_ref.refs_2_, s32[8,7]{1,0:T(8,128)} %columns_ref.1, f32[8,64,448]{2,1,0:T(8,128)} %a_ref.1), custom_call_target="tpu_custom_call" | custom-call | flops 99999997952 | bytes 4000 | tf_op jit(solution)/shard_map/left_product/pallas_call | solution.py:172
  18.9 0.0 collective-permute-done.2.refs_5_
  18.9 1.6 %collective-permute-start.7 = (f32[2,64,256]{2,1,0:T(8,128)S(1)}, f32[2,64,256]{2,1,0:T(8,128)S(1)}, u32[]{:S(2)}, u32[]{:S(2)}) collective-permute-start(f32[2,64,256]{2,1,0:T(8,128)S(1)} %collective-permute-done.2.refs_5_), channel_id=1, source_target_pairs={{0,2},{1,7},{2,4},{3,1},{4,6},{5,3},{6,0},{7,5},{8,10},{9,15},{10,... | collective-permute-start | bytes 393224 | tf_op jit(solution)/shard_map/ppermute | solution.py:367
  20.5 0.7 %turned.1 = (bf16[5,256,512]{2,1,0:T(8,128)(2,1)S(1)}, bf16[5,256,512]{2,1,0:T(8,128)(2,1)S(1)}) custom-call(f32[2560,256]{1,0:T(8,128)S(1)} %left_product.1.left_ref), custom_call_target="tpu_custom_call" | custom-call | flops 1000000000 | bytes 5000 | tf_op jit(solution)/shard_map/turned/pallas_call | solution.py:197
  21.3 1.4 %products.2.refs_0_ = f32[4,64,1280]{2,1,0:T(8,128)} custom-call(bf16[5,256,512]{2,1,0:T(8,128)(2,1)S(1)} %get-tuple-element.12.refs_0_.refs_1_.high_ref, bf16[5,256,512]{2,1,0:T(8,128)(2,1)S(1)} %get-tuple-element.13.refs_1_.refs_2_.low_ref, f32[8,64,256]{2,1,0:T(8,128)S(1)} %get-tuple-element.11.dense_ref.refs_2_, ...), custom_call_target="tpu_custom_call" | custom-call | flops 200000000 | bytes 2000 | tf_op jit(solution)/shard_map/products/pallas_call | solution.py:245
  22.7 0.0 collective-permute-done.5.refs_0_
  22.7 0.3 partial_product.2.refs_0_
  23.0 1.0 %collective-permute-done.6.refs_1_ = f32[3,64,256]{2,1,0:T(8,128)S(1)} collective-permute-done((f32[3,64,256]{2,1,0:T(8,128)S(1)}, f32[3,64,256]{2,1,0:T(8,128)S(1)}, u32[]{:S(2)}, u32[]{:S(2)}) %collective-permute-start.6) | collective-permute-done | bytes 196640 | tf_op jit(solution)/shard_map/ppermute | solution.py:367
  24.0 0.3 %partial_product.3.before_ref = f32[4,64,256]{2,1,0:T(8,128)S(1)} custom-call(bf16[5,256,512]{2,1,0:T(8,128)(2,1)S(1)} %get-tuple-element.12.refs_0_.refs_1_.high_ref, bf16[5,256,512]{2,1,0:T(8,128)(2,1)S(1)} %get-tuple-element.13.refs_1_.refs_2_.low_ref, f32[4,64,256]{2,1,0:T(8,128)S(1)} %partial_product.2.refs_0_, ...), custom_call_target="tpu_custom_call" | custom-call | flops 1000 | bytes 1500 | tf_op jit(solution)/shard_map/partial_product/pallas_call | solution.py:272
  24.3 0.0 collective-permute-done.3.refs_3_
  24.3 0.0 collective-permute-done.4.refs_4_
  24.3 1.4 %products.3.out_in_ref = f32[4,64,1280]{2,1,0:T(8,128)} custom-call(f32[4,64,1280]{2,1,0:T(8,128)} %products.2.refs_0_, bf16[5,256,512]{2,1,0:T(8,128)(2,1)S(1)} %get-tuple-element.12.refs_0_.refs_1_.high_ref, bf16[5,256,512]{2,1,0:T(8,128)(2,1)S(1)} %get-tuple-element.13.refs_1_.refs_2_.low_ref, ...), custom_call_target="tpu_custom_call", output_to_operand_aliasing={{}: (0, {})} | custom-call | flops 200000000 | bytes 2000 | tf_op jit(solution)/shard_map/products/pallas_call | solution.py:245
  25.7 0.0 collective-permute-done.7.part_ref
  25.7 1.0 %last_product.1 = f32[4,64,1280]{2,1,0:T(8,128)} custom-call(f32[4,64,1280]{2,1,0:T(8,128)} %products.3.out_in_ref, bf16[5,256,512]{2,1,0:T(8,128)(2,1)S(1)} %get-tuple-element.12.refs_0_.refs_1_.high_ref, bf16[5,256,512]{2,1,0:T(8,128)(2,1)S(1)} %get-tuple-element.13.refs_1_.refs_2_.low_ref, ...), custom_call_target="tpu_custom_call", output_to_operand_aliasing={{}: (0, {})} | custom-call | flops 1000 | bytes 700 | tf_op jit(solution)/shard_map/last_product/pallas_call | solution.py:290
Async XLA Ops:
  1.3 8.7 %collective-permute-start = (f32[3,64,256]{2,1,0:T(8,128)S(1)}, f32[3,64,256]{2,1,0:T(8,128)S(1)}, u32[]{:S(2)}, u32[]{:S(2)}) collective-permute-start(f32[3,64,256]{2,1,0:T(8,128)S(1)} %get-tuple-element.14), channel_id=1, source_target_pairs={{0,1},{1,0},{2,3},{3,2},{4,5},{5,4},{6,7},{7,6},{8,9},{9,8},{10,11... | collective-permute-start | bytes 589832 | tf_op jit(solution)/shard_map/ppermute | solution.py:349
  4.3 9.9 %collective-permute-start.1 = (f32[3,64,256]{2,1,0:T(8,128)S(1)}, f32[3,64,256]{2,1,0:T(8,128)S(1)}, u32[]{:S(2)}, u32[]{:S(2)}) collective-permute-start(f32[3,64,256]{2,1,0:T(8,128)S(1)} %get-tuple-element.15), channel_id=1, source_target_pairs={{0,1},{1,0},{2,3},{3,2},{4,5},{5,4},{6,7},{7,6},{8,9},{9,8},{10,11... | collective-permute-start | bytes 589832 | tf_op jit(solution)/shard_map/ppermute | solution.py:349
  4.4 19.9 %collective-permute-start.3 = (f32[8,64,256]{2,1,0:T(8,128)S(1)}, f32[8,64,256]{2,1,0:T(8,128)S(1)}, u32[]{:S(2)}, u32[]{:S(2)}) collective-permute-start(f32[8,64,256]{2,1,0:T(8,128)S(1)} %get-tuple-element.11.dense_ref.refs_2_), channel_id=1, source_target_pairs={{0,8},{8,0},{16,24},{24,16},{1,9},{9,1},{17,25},{25,17},{2,10},{10... | collective-permute-start | bytes 1572872 | tf_op jit(solution)/shard_map/ppermute | solution.py:376
  4.4 19.9 %collective-permute-start.4 = (f32[8,64,256]{2,1,0:T(8,128)S(1)}, f32[8,64,256]{2,1,0:T(8,128)S(1)}, u32[]{:S(2)}, u32[]{:S(2)}) collective-permute-start(f32[8,64,256]{2,1,0:T(8,128)S(1)} %get-tuple-element.11.dense_ref.refs_2_), channel_id=1, source_target_pairs={{8,16},{16,8},{9,17},{17,9},{10,18},{18,10},{11,19},{19,11},{12,20... | collective-permute-start | bytes 1572872 | tf_op jit(solution)/shard_map/ppermute | solution.py:377
  5.1 13.8 %collective-permute-start.2 = (f32[2,64,256]{2,1,0:T(8,128)S(1)}, f32[2,64,256]{2,1,0:T(8,128)S(1)}, u32[]{:S(2)}, u32[]{:S(2)}) collective-permute-start(f32[2,64,256]{2,1,0:T(8,128)S(1)} %get-tuple-element.16), channel_id=1, source_target_pairs={{0,1},{1,0},{2,3},{3,2},{4,5},{5,4},{6,7},{7,6},{8,9},{9,8},{10,11... | collective-permute-start | bytes 393224 | tf_op jit(solution)/shard_map/ppermute | solution.py:349
  10.1 12.6 %collective-permute-start.5 = (f32[3,64,256]{2,1,0:T(8,128)S(1)}, f32[3,64,256]{2,1,0:T(8,128)S(1)}, u32[]{:S(2)}, u32[]{:S(2)}) collective-permute-start(f32[3,64,256]{2,1,0:T(8,128)S(1)} %collective-permute-done.refs_3_), channel_id=1, source_target_pairs={{0,2},{1,7},{2,4},{3,1},{4,6},{5,3},{6,0},{7,5},{8,10},{9,15},{10,... | collective-permute-start | bytes 589832 | tf_op jit(solution)/shard_map/ppermute | solution.py:367
  14.3 9.7 %collective-permute-start.6 = (f32[3,64,256]{2,1,0:T(8,128)S(1)}, f32[3,64,256]{2,1,0:T(8,128)S(1)}, u32[]{:S(2)}, u32[]{:S(2)}) collective-permute-start(f32[3,64,256]{2,1,0:T(8,128)S(1)} %collective-permute-done.1.refs_4_), channel_id=1, source_target_pairs={{0,2},{1,7},{2,4},{3,1},{4,6},{5,3},{6,0},{7,5},{8,10},{9,15},{10,... | collective-permute-start | bytes 589832 | tf_op jit(solution)/shard_map/ppermute | solution.py:367
  18.9 6.8 %collective-permute-start.7 = (f32[2,64,256]{2,1,0:T(8,128)S(1)}, f32[2,64,256]{2,1,0:T(8,128)S(1)}, u32[]{:S(2)}, u32[]{:S(2)}) collective-permute-start(f32[2,64,256]{2,1,0:T(8,128)S(1)} %collective-permute-done.2.refs_5_), channel_id=1, source_target_pairs={{0,2},{1,7},{2,4},{3,1},{4,6},{5,3},{6,0},{7,5},{8,10},{9,15},{10,... | collective-permute-start | bytes 393224 | tf_op jit(solution)/shard_map/ppermute | solution.py:367
where the time goes:
time: 26.9 us; the launch traced here: 26.7 us
  starting transfers between devices  11.7 us (43%)
  Pallas kernels  8.85 us (33%)
  waiting for transfers between devices  6.06 us (23%)
    ppermute x3, starting transfers between devices, per_device(): far.append(lax.ppermute(part, 'col', onward))  5.92 us
    ppermute x3, starting transfers between devices, per_device(): pair.append(lax.ppermute(part, 'col', pairs))  5.09 us
    ppermute x3, waiting for transfers between devices, per_device(): pair.append(lax.ppermute(part, 'col', pairs))  5.02 us
    pallas_call x2, Pallas kernels, products(): pl.pallas_call(functools.partial(products_kernel, places, counts, len(giv...  2.8 us
    pallas_call x1, Pallas kernels, left_product(): pl.pallas_call(functools.partial(left_kernel, col_count, first), in_specs...  2.44 us
    pallas_call x1, Pallas kernels, dense_rows(): pl.pallas_call(dense_kernel, in_specs=[HBM] * 4, out_specs=[VMEM] * (len(...  1.33 us
    ppermute x3, waiting for transfers between devices, per_device(): far.append(lax.ppermute(part, 'col', onward))  1.03 us
    pallas_call x1, Pallas kernels, last_product(): pl.pallas_call(functools.partial(last_kernel, place, at), in_specs=[HBM]...  0.97 us
  transfers between devices with their start and end apart: 8, of which 3 were waited for; matrix products, arithmetic and copies ran while one was open for 0% of the time, Pallas kernels for 25%

commit v1 on v0

--- a/solution.py
+++ b/solution.py
@@ -7,7 +7,7 @@
 from jax.experimental.pallas import tpu as pltpu
 from jax.sharding import PartitionSpec as P
 
-CFG = {'parts': (3, 3, 2), 'xg': 0, 'la': None, 'tick': 1, 'ck': 100000000, 'gk': (2,), 'gf': (), 'rg': None, 'rs': 1, 'pr': 2, 'ch': 1, 'cl': 100000000000, 'ct': 1000000000, 'cp': 100000000, 'ca': 1000, 'cz': 1000, 'cut': 8, 'lb': None, 'g1': []}
+CFG = {'parts': (2, 3, 3), 'x3': 'f', 'lrc': 1, 'la': 0, 'tick': 1, 'ck': 100000000000, 'gk': (0, 2), 'gr': 'tick', 'gf': (1, 2), 'rg': None, 'cut': 8, 'pr': ((0, 1), (3, 4)), 'fo': (0, 1, 2), 'fl': [1], 'cl': 100000000, 'ct': 1000, 'cp': 100000000, 'ca': 1000000000, 'cz': 100000000}
 
 BS = 64
 KA = 7
@@ -223,81 +223,55 @@
     return total.reshape(CA, BS, WIDE)
 
 
-def products_kernel(places, counts, given, *refs):
-    high_ref, low_ref, *refs = refs[given:]
-    part_refs = refs[: sum(counts)]
-    out_ref, blocks, sems = refs[sum(counts) :]
+def stage_kernel(has_out, flushed, sums, final, *refs):
+    refs = list(refs)
+    out_in_ref = refs.pop(0) if has_out else None
+    del out_in_ref
+    high_ref, low_ref = refs.pop(0), refs.pop(0)
+    flush_refs = [refs.pop(0) for _ in flushed]
+    given = [([refs.pop(0) for _ in range(1 if has_before else 0)], [refs.pop(0) for _ in range(count)]) for _, count, _, has_before in sums]
+    out_ref = refs.pop(0) if flushed or final else None
+    total_refs = [refs.pop(0) for _ in sums]
+    sems = refs.pop(0)
     groups = groups_here()
-    copies = []
-    for index, place in enumerate(places):
-        at = sum(counts[:index])
-        blocks[index] = summed(high_ref, low_ref, place, part_refs[at : at + counts[index]])
-        copies.append(put_block(groups[place], blocks.at[index], out_ref, sems.at[index]))
+    copies = [put_block(groups[place], ref, out_ref, sems.at[i]) for i, (place, ref) in enumerate(zip(flushed, flush_refs))]
+    for (place, _, at, _), (before, parts), total_ref in zip(sums, given, total_refs):
+        total = summed(high_ref, low_ref, place, parts, at)
+        total_ref[...] = before[0][...] + total if before else total
+        if final:
+            copies.append(put_block(groups[place], total_ref, out_ref, sems.at[len(copies)]))
     for copy in copies:
         copy.wait()
 
 
-def products(out, high, low, parts):
-    places = tuple(parts)
-    counts = tuple(len(parts[place]) for place in places)
-    flat = [part for place in places for part in parts[place]]
-    given = [] if out is None else [out]
-    return pl.pallas_call(
-        functools.partial(products_kernel, places, counts, len(given)),
-        in_specs=[HBM] * len(given) + [VMEM] * (2 + len(flat)),
-        out_specs=HBM,
-        out_shape=jax.ShapeDtypeStruct((CA, BS, 5 * WIDE), jnp.float32),
-        scratch_shapes=[
-            pltpu.VMEM((len(places), CA, BS, WIDE), jnp.float32),
-            pltpu.SemaphoreType.DMA((len(places),)),
-        ],
-        input_output_aliases={0: 0} if given else {},
+def stage(out, high, low, flush, sums, flops, final=False):
+    writes = bool(flush) or final
+    given_out = [out] if writes and out is not None else []
+    shapes = [jax.ShapeDtypeStruct((CA, BS, 5 * WIDE), jnp.float32)] if writes else []
+    block = (CA, BS, WIDE)
+    flat = list(flush.values())
+    for parts, _, before in sums.values():
+        flat += ([] if before is None else [before]) + parts
+    plan = tuple((place, len(parts), at, before is not None) for place, (parts, at, before) in sums.items())
+    scratch = [pltpu.SemaphoreType.DMA((max(1, len(flush) + len(sums)),))]
+    if final:
+        scratch = [pltpu.VMEM(block, jnp.float32)] * len(sums) + scratch
+    else:
+        shapes += [pltpu.VMEM(block, jnp.float32)] * len(sums)
+    totals = pl.pallas_call(
+        functools.partial(stage_kernel, bool(given_out), tuple(flush), plan, final),
+        in_specs=[HBM] * len(given_out) + [VMEM] * (2 + len(flat)),
+        out_specs=[HBM] * writes + [VMEM] * (len(shapes) - writes),
+        out_shape=shapes,
+        scratch_shapes=scratch,
+        input_output_aliases={0: 0} if given_out else {},
         compiler_params=pltpu.CompilerParams(vmem_limit_bytes=16 * MIB),
-        cost_estimate=cost(CFG['cp'] * len(places), 2000),
-        name="products",
-    )(*given, *map(in_vmem, (high, low, *flat)))
-
-
-def partial_kernel(place, at, chained, high_ref, low_ref, *refs):
-    part_refs = refs[:-1]
-    if chained:
-        before_ref, *part_refs = part_refs
-        refs[-1][...] = before_ref[...] + summed(high_ref, low_ref, place, part_refs, at)
-    else:
-        refs[-1][...] = summed(high_ref, low_ref, place, part_refs, at)
-
-
-def partial_product(high, low, before, parts, place, at):
-    given = [] if before is None else [before]
-    return pl.pallas_call(
-        functools.partial(partial_kernel, place, at, bool(given)),
-        in_specs=[VMEM] * (2 + len(given) + len(parts)),
-        out_specs=VMEM,
-        out_shape=pltpu.VMEM((CA, BS, WIDE), jnp.float32),
-        compiler_params=pltpu.CompilerParams(vmem_limit_bytes=16 * MIB),
-        cost_estimate=cost(CFG['ca'], 1500),
-        name="partial_product",
-    )(*map(in_vmem, (high, low, *given, *parts)))
-
-
-def last_kernel(place, at, out_in_ref, high_ref, low_ref, before_ref, part_ref, out_ref, block, sem):
-    del out_in_ref
-    block[...] = before_ref[...] + summed(high_ref, low_ref, place, [part_ref], at)
-    put_block(groups_here()[place], block, out_ref, sem).wait()
-
-
-def last_product(out, high, low, before, part, place, at):
-    return pl.pallas_call(
-        functools.partial(last_kernel, place, at),
-        in_specs=[HBM] + [VMEM] * 4,
-        out_specs=HBM,
-        out_shape=jax.ShapeDtypeStruct(out.shape, out.dtype),
-        scratch_shapes=[pltpu.VMEM((CA, BS, WIDE), jnp.float32), pltpu.SemaphoreType.DMA],
-        input_output_aliases={0: 0},
-        compiler_params=pltpu.CompilerParams(vmem_limit_bytes=16 * MIB),
-        cost_estimate=cost(CFG['cz'], 700),
-        name="last_product",
-    )(out, *map(in_vmem, (high, low, before, part)))
+        cost_estimate=cost(flops, 2000),
+        name="last_product" if final else "stage%d%sf%d" % (len(sums), "p" if plan[0][0] == FAR_COL else "", len(flush)),
+    )(*given_out, *map(in_vmem, (high, low, *flat)))
+    if writes:
+        out, *totals = totals
+    return out, dict(zip(sums, totals))
 
 
 def column_pairs(count):
@@ -312,9 +286,12 @@
     return [(i, i ^ 1) for i in range(count)]
 
 
-def row_between(count):
-    pairs = [(i, i + 1) for i in range(1, count - 1, 2)]
-    return pairs + [(b, a) for a, b in pairs]
+def beyond(count):
+    return [(i, (i + 1) % count if i % 2 else (i - 1) % count) for i in range(count)]
+
+
+def two_on(count):
+    return [(i, (i + 2) % count if i % 2 else (i - 2) % count) for i in range(count)]
 
 
 def after(value, *others):
@@ -339,62 +316,60 @@
 def per_device(a_values, a_columns, p_values, p_columns, p_count, aggregates):
     row_count = lax.axis_size("row")
     col_count = lax.axis_size("col")
-    depth = a_values.shape[0] * BS
+    rows = a_values.shape[0]
     pairs, onward = column_pairs(col_count), column_onward(col_count)
     parts, dense = dense_rows(p_values, p_columns, p_count, aggregates)
-    pair, far = [], []
+    ticked = tick(parts[0], CFG['ck']) if CFG['tick'] else None
+    direct = lax.ppermute(parts[-1], "col", two_on(col_count))
+    to_row = dense
+    if CFG['rg'] == 'tick' and CFG['tick']:
+        to_row = after(dense, ticked)
+    pair_row = lax.ppermute(dense, "row", row_pairs(row_count))
+    far_row = lax.ppermute(to_row, "row", beyond(row_count))
+    pair = []
     for index, part in enumerate(parts):
-        if CFG['xg'] and index >= CFG['xg']:
-            part = after(part, pair[index - CFG['xg']])
+        if index == len(parts) - 1 and CFG['x3'] == 'f':
+            part = after(part, pair[0])
+        elif index == len(parts) - 1 and CFG['x3'] == 'd':
+            part = after(part, direct)
+        elif index == len(parts) - 1 and CFG['x3'] == 'r':
+            part = after(part, pair_row)
         pair.append(lax.ppermute(part, "col", pairs))
     own = dense
+    if CFG['lrc']:
+        own = after(own, pair_row)
     if CFG['la'] is not None:
-        own = after(dense, pair[CFG['la']])
-    cut = CFG['cut']
-    rows = a_values.shape[0]
-    left = first = left_product(own, a_columns, a_values, None, 0, cut, col_count)
-    if cut < rows:
-        again = dense if CFG['lb'] is None else after(dense, pair[min(CFG['lb'], len(pair) - 1)])
-        left = left_product(again, a_columns, a_values, first, cut, rows - cut, col_count)
-    ticked = tick(parts[0], CFG['ck']) if CFG['tick'] else None
-    for index, part in enumerate(pair):
+        own = after(own, pair[CFG['la']])
+    left = left_product(own, a_columns, a_values, None, 0, rows, col_count)
+    far = []
+    for index, part in enumerate(pair[:-1]):
         if index in CFG['gf']:
             part = after(part, left)
-        if index in CFG['g1']:
-            part = after(part, first)
         if CFG['tick'] and index in CFG['gk']:
             part = after(part, ticked)
         far.append(lax.ppermute(part, "col", onward))
-    to_row = dense
-    if CFG['rg'] == 'left':
-        to_row = after(dense, left)
-    elif CFG['rg'] == 'tick' and CFG['tick']:
-        to_row = after(dense, ticked)
-    elif isinstance(CFG['rg'], int):
-        to_row = after(dense, pair[CFG['rg']])
-    if CFG['rs']:
-        pair_row = lax.ppermute(to_row, "row", row_pairs(row_count))
-        far_row = lax.ppermute(to_row, "row", row_between(row_count))
-    else:
-        far_row = lax.ppermute(to_row, "row", row_between(row_count))
-        pair_row = lax.ppermute(to_row, "row", row_pairs(row_count))
+    if CFG['gr'] == 'left':
+        direct = after(direct, left)
+    elif CFG['gr'] == 'tick' and CFG['tick']:
+        direct = after(direct, ticked)
+    far.append(lax.ppermute(direct, "col", pairs))
     high, low = turned(left)
-    if CFG['pr'] == 0:
-        out = products(None, high, low, {OWN: [dense], PAIR_ROW: [pair_row], FAR_ROW: [far_row], PAIR_COL: pair})
-    elif CFG['pr'] == 1:
-        out = products(None, high, low, {OWN: [dense], PAIR_ROW: [pair_row], FAR_ROW: [far_row]})
-        out = products(out, high, low, {PAIR_COL: pair})
-    elif CFG['pr'] == 2:
-        out = products(None, high, low, {OWN: [dense], PAIR_COL: pair})
-        out = products(out, high, low, {PAIR_ROW: [pair_row], FAR_ROW: [far_row]})
-    if CFG['ch']:
-        before, at = None, 0
-        for part in far[:-1]:
-            before = partial_product(high, low, before, [part], FAR_COL, at)
-            at += part.shape[0] * BS
-    else:
-        before = partial_product(high, low, None, far[:-1], FAR_COL, 0)
-    return last_product(out, high, low, before, far[-1], FAR_COL, depth - PARTS[-1] * BS)
+    given = {OWN: [dense], PAIR_ROW: [pair_row], FAR_ROW: [far_row], PAIR_COL: pair}
+    ats = [sum(PARTS[:k]) * BS for k in range(len(PARTS))]
+    steps = [{place: (given[place], 0) for place in group} for group in CFG['pr']]
+    steps += [{FAR_COL: ([far[k]], ats[k])} for k in CFG['fo']]
+    out, ready, before = None, {}, None
+    for step, what in enumerate(steps):
+        last = step == len(steps) - 1
+        now = step in CFG['fl'] or last
+        sums = {place: (*some, before if place == FAR_COL else None) for place, some in what.items()}
+        flops = CFG['cz'] if last else CFG['ca'] if FAR_COL in what else CFG['cp']
+        out, totals = stage(out, high, low, ready if now else {}, sums, flops, last)
+        ready = {} if now else ready
+        if not last:
+            before = totals.pop(FAR_COL, before)
+            ready = {**ready, **totals}
+    return out
 
 
 def solution(mesh):

time: 26.9 us -> 23.6 us (0.88)
  waiting for transfers between devices: 6.06 us -> 1.37 us
  starting transfers between devices: 11.7 us -> 14.1 us
  Pallas kernels: 8.85 us -> 7.85 us
    ppermute x2 -> x4, starting transfers between devices: 0.69 us -> 7.44 us  [the longest x1 3.6 us: per_device(): direct = lax.ppermute(parts[-1], 'col', two_on(col_count))]
    ppermute x3, waiting for transfers between devices: 5.02 us -> 0.01 us  [per_device(): pair.append(lax.ppermute(part, 'col', pairs))]
    ppermute x3 -> x2, starting transfers between devices: 5.92 us -> 3.1 us  [per_device(): far.append(lax.ppermute(part, 'col', onward))]
    ppermute x3, starting transfers between devices: 5.09 us -> 3.54 us  [per_device(): pair.append(lax.ppermute(part, 'col', pairs))]
    pallas_call x5, Pallas kernels: 4.34 us -> 3.37 us  [stage(): pl.pallas_call(functools.partial(stage_kernel, bool(given_out), tuple(flu...]
    ppermute x3 -> x2, waiting for transfers between devices: 1.03 us -> 1.35 us  [per_device(): far.append(lax.ppermute(part, 'col', onward))]
  transfers between devices with their start and end apart: 8 -> 9, of which waited for: 3 -> 1; matrix products, arithmetic and copies ran while one was open for 0% -> 0% of each run, Pallas kernels for 25% -> 23%
where the time goes in v1:
time: 23.6 us; the launch traced here: 23.4 us
  starting transfers between devices  14.1 us (60%)
  Pallas kernels  7.85 us (33%)
  waiting for transfers between devices  1.37 us (6%)
    ppermute x1, starting transfers between devices, per_device(): direct = lax.ppermute(parts[-1], 'col', two_on(col_count))  3.6 us
    ppermute x3, starting transfers between devices, per_device(): pair.append(lax.ppermute(part, 'col', pairs))  3.54 us
    pallas_call x5, Pallas kernels, stage(): pl.pallas_call(functools.partial(stage_kernel, bool(given_out), tuple(flu...  3.37 us
    ppermute x2, starting transfers between devices, per_device(): far.append(lax.ppermute(part, 'col', onward))  3.1 us
    pallas_call x1, Pallas kernels, left_product(): pl.pallas_call(functools.partial(left_kernel, col_count, first), in_specs...  2.43 us
    ppermute x1, starting transfers between devices, per_device(): far.append(lax.ppermute(direct, 'col', pairs))  2.2 us
    ppermute x1, starting transfers between devices, per_device(): far_row = lax.ppermute(to_row, 'row', beyond(row_count))  1.63 us
    ppermute x2, waiting for transfers between devices, per_device(): far.append(lax.ppermute(part, 'col', onward))  1.35 us
  transfers between devices with their start and end apart: 9, of which 1 were waited for; matrix products, arithmetic and copies ran while one was open for 0% of the time, Pallas kernels for 23%

profile of v1, /device:TPU:0, one launch (start us, length us, event | category | flops | bytes accessed | tf_op | source)
XLA Modules:
  0.0 23.4 jit_solution(214512686551528442)
XLA Ops:
  0.0 1.3 %dense_rows.1 = (f32[2,64,256]{2,1,0:T(8,128)S(1)}, f32[3,64,256]{2,1,0:T(8,128)S(1)}, f32[3,64,256]{2,1,0:T(8,128)S(1)}, f32[8,64,256]{2,1,0:T(8,128)S(1)}) custom-call(f32[8,64,256]{2,1,0:T(8,128)} %values_ref.1, s32[4,8]{1,0:T(4,128)} %bitcast.1, s32[8]{0:T(128)} %counts_ref.1, s32[8]{0:T(128)} %aggregates_ref.1), custom_call_target="tpu_custom_call" | custom-call | flops 400000 | bytes 1572864 | tf_op jit(solution)/shard_map/dense_rows/pallas_call | solution.py:106
  1.3 3.0 %collective-permute-start.1 = (f32[2,64,256]{2,1,0:T(8,128)S(1)}, f32[2,64,256]{2,1,0:T(8,128)S(1)}, u32[]{:S(2)}, u32[]{:S(2)}) collective-permute-start(f32[2,64,256]{2,1,0:T(8,128)S(1)} %get-tuple-element.24), channel_id=1, source_target_pairs={{0,1},{1,0},{2,3},{3,2},{4,5},{5,4},{6,7},{7,6},{8,9},{9,8},{10,11... | collective-permute-start | bytes 393224 | tf_op jit(solution)/shard_map/ppermute | solution.py:337
  4.3 0.0 collective-permute-start
  4.3 1.6 %collective-permute-start.4 = (f32[8,64,256]{2,1,0:T(8,128)S(1)}, f32[8,64,256]{2,1,0:T(8,128)S(1)}, u32[]{:S(2)}, u32[]{:S(2)}) collective-permute-start(f32[8,64,256]{2,1,0:T(8,128)S(1)} %get-tuple-element.25.dense_ref.refs_2_), channel_id=1, source_target_pairs={{0,24},{8,16},{16,8},{24,0},{1,25},{9,17},{17,9},{25,1},{2,26},{10... | collective-permute-start | bytes 1572872 | tf_op jit(solution)/shard_map/ppermute | solution.py:328
  6.0 0.5 %collective-permute-start.2 = (f32[3,64,256]{2,1,0:T(8,128)S(1)}, f32[3,64,256]{2,1,0:T(8,128)S(1)}, u32[]{:S(2)}, u32[]{:S(2)}) collective-permute-start(f32[3,64,256]{2,1,0:T(8,128)S(1)} %get-tuple-element.28), channel_id=1, source_target_pairs={{0,1},{1,0},{2,3},{3,2},{4,5},{5,4},{6,7},{7,6},{8,9},{9,8},{10,11... | collective-permute-start | bytes 589832 | tf_op jit(solution)/shard_map/ppermute | solution.py:337
  6.5 3.6 %collective-permute-start.7 = (f32[3,64,256]{2,1,0:T(8,128)S(1)}, f32[3,64,256]{2,1,0:T(8,128)S(1)}, u32[]{:S(2)}, u32[]{:S(2)}) collective-permute-start(f32[3,64,256]{2,1,0:T(8,128)S(1)} %get-tuple-element.30), channel_id=1, source_target_pairs={{0,6},{1,3},{2,0},{3,5},{4,2},{5,7},{6,4},{7,1},{8,14},{9,11},{10,... | collective-permute-start | bytes 589832 | tf_op jit(solution)/shard_map/ppermute | solution.py:323
  10.1 0.0 collective-permute-done.1.refs_3_
  10.1 0.0 collective-permute-start.3
  10.1 0.0 collective-permute-done.refs_4_
  10.1 1.5 %collective-permute-start.5 = (f32[2,64,256]{2,1,0:T(8,128)S(1)}, f32[2,64,256]{2,1,0:T(8,128)S(1)}, u32[]{:S(2)}, u32[]{:S(2)}) collective-permute-start(f32[2,64,256]{2,1,0:T(8,128)S(1)} %collective-permute-done.1.refs_3_), channel_id=1, source_target_pairs={{0,2},{1,7},{2,4},{3,1},{4,6},{5,3},{6,0},{7,5},{8,10},{9,15},{10,... | collective-permute-start | bytes 393224 | tf_op jit(solution)/shard_map/ppermute | solution.py:350
  11.6 2.4 %left_product.1.left_ref = f32[2560,256]{1,0:T(8,128)S(1)} custom-call(f32[8,64,256]{2,1,0:T(8,128)S(1)} %get-tuple-element.25.dense_ref.refs_2_, s32[8,7]{1,0:T(8,128)} %columns_ref.1, f32[8,64,448]{2,1,0:T(8,128)} %a_ref.1), custom_call_target="tpu_custom_call" | custom-call | flops 100000000 | bytes 4000 | tf_op jit(solution)/shard_map/left_product/pallas_call | solution.py:172
  14.0 0.0 collective-permute-done.2.refs_4_
  14.0 1.6 %collective-permute-start.6 = (f32[3,64,256]{2,1,0:T(8,128)S(1)}, f32[3,64,256]{2,1,0:T(8,128)S(1)}, u32[]{:S(2)}, u32[]{:S(2)}) collective-permute-start(f32[3,64,256]{2,1,0:T(8,128)S(1)} %collective-permute-done.2.refs_4_), channel_id=1, source_target_pairs={{0,2},{1,7},{2,4},{3,1},{4,6},{5,3},{6,0},{7,5},{8,10},{9,15},{10,... | collective-permute-start | bytes 589832 | tf_op jit(solution)/shard_map/ppermute | solution.py:350
  15.7 0.0 collective-permute-done.7
  15.7 2.2 %collective-permute-start.8 = (f32[3,64,256]{2,1,0:T(8,128)S(1)}, f32[3,64,256]{2,1,0:T(8,128)S(1)}, u32[]{:S(2)}, u32[]{:S(2)}) collective-permute-start(f32[3,64,256]{2,1,0:T(8,128)S(1)} %collective-permute-done.7), channel_id=1, source_target_pairs={{0,1},{1,0},{2,3},{3,2},{4,5},{5,4},{6,7},{7,6},{8,9},{9,8},{10,11... | collective-permute-start | bytes 589832 | tf_op jit(solution)/shard_map/ppermute | solution.py:355
  17.9 0.7 %turned.1 = (bf16[5,256,512]{2,1,0:T(8,128)(2,1)S(1)}, bf16[5,256,512]{2,1,0:T(8,128)(2,1)S(1)}) custom-call(f32[2560,256]{1,0:T(8,128)S(1)} %left_product.1.left_ref), custom_call_target="tpu_custom_call" | custom-call | flops 1000 | bytes 5000 | tf_op jit(solution)/shard_map/turned/pallas_call | solution.py:197
  18.6 0.0 collective-permute-done.3.refs_5_
  18.6 0.7 %stage2f0.1 = (f32[4,64,256]{2,1,0:T(8,128)S(1)}, f32[4,64,256]{2,1,0:T(8,128)S(1)}) custom-call(bf16[5,256,512]{2,1,0:T(8,128)(2,1)S(1)} %get-tuple-element.26.refs_0_.refs_1_, bf16[5,256,512]{2,1,0:T(8,128)(2,1)S(1)} %get-tuple-element.27.refs_1_.refs_2_, f32[8,64,256]{2,1,0:T(8,128)S(1)} %get-tuple-element.25.dense_ref.refs_2_, ...), custom_call_target="tpu_custom_call" | custom-call | flops 100000000 | bytes 2000 | tf_op jit(solution)/shard_map/stage2f0/pallas_call | solution.py:261
  19.3 0.0 collective-permute-done.4.refs_5_
  19.3 1.1 %stage2f2.1 = (f32[4,64,1280]{2,1,0:T(8,128)}, f32[4,64,256]{2,1,0:T(8,128)S(1)}, f32[4,64,256]{2,1,0:T(8,128)S(1)}) custom-call(bf16[5,256,512]{2,1,0:T(8,128)(2,1)S(1)} %get-tuple-element.26.refs_0_.refs_1_, bf16[5,256,512]{2,1,0:T(8,128)(2,1)S(1)} %get-tuple-element.27.refs_1_.refs_2_, f32[4,64,256]{2,1,0:T(8,128)S(1)} %get-tuple-element.31.refs_2_, ...), custom_call_target="tpu_custom_call" | custom-call | flops 100000000 | bytes 2000 | tf_op jit(solution)/shard_map/stage2f2/pallas_call | solution.py:261
  20.4 0.0 collective-permute-done.5.refs_2_
  20.4 0.3 %stage1pf0.2.refs_2_ = f32[4,64,256]{2,1,0:T(8,128)S(1)} custom-call(bf16[5,256,512]{2,1,0:T(8,128)(2,1)S(1)} %get-tuple-element.26.refs_0_.refs_1_, bf16[5,256,512]{2,1,0:T(8,128)(2,1)S(1)} %get-tuple-element.27.refs_1_.refs_2_, f32[2,64,256]{2,1,0:T(8,128)S(1)} %collective-permute-done.5.refs_2_), custom_call_target="tpu_custom_call" | custom-call | flops 1000000000 | bytes 2000 | tf_op jit(solution)/shard_map/stage1pf0/pallas_call | solution.py:261
  20.7 1.3 %collective-permute-done.6.refs_3_ = f32[3,64,256]{2,1,0:T(8,128)S(1)} collective-permute-done((f32[3,64,256]{2,1,0:T(8,128)S(1)}, f32[3,64,256]{2,1,0:T(8,128)S(1)}, u32[]{:S(2)}, u32[]{:S(2)}) %collective-permute-start.6) | collective-permute-done | bytes 196640 | tf_op jit(solution)/shard_map/ppermute | solution.py:350
  22.1 0.3 %stage1pf0.3.refs_5_ = f32[4,64,256]{2,1,0:T(8,128)S(1)} custom-call(bf16[5,256,512]{2,1,0:T(8,128)(2,1)S(1)} %get-tuple-element.26.refs_0_.refs_1_, bf16[5,256,512]{2,1,0:T(8,128)(2,1)S(1)} %get-tuple-element.27.refs_1_.refs_2_, f32[4,64,256]{2,1,0:T(8,128)S(1)} %stage1pf0.2.refs_2_, f32[3,64,256]{2,1,0:T(8,128)S(1)} %collective-permute-done.6.refs_3_), custom_call_target="tpu_custom_call" | custom-call | flops 1000000000 | bytes 2000 | tf_op jit(solution)/shard_map/stage1pf0/pallas_call | solution.py:261
  22.4 0.0 collective-permute-done.8.refs_6_
  22.4 1.0 %last_product.1 = f32[4,64,1280]{2,1,0:T(8,128)} custom-call(f32[4,64,1280]{2,1,0:T(8,128)} %get-tuple-element.33.refs_0_, bf16[5,256,512]{2,1,0:T(8,128)(2,1)S(1)} %get-tuple-element.26.refs_0_.refs_1_, bf16[5,256,512]{2,1,0:T(8,128)(2,1)S(1)} %get-tuple-element.27.refs_1_.refs_2_, ...), custom_call_target="tpu_custom_call", output_to_operand_aliasing={{}: (0, {})} | custom-call | flops 100000000 | bytes 2000 | tf_op jit(solution)/shard_map/last_product/pallas_call | solution.py:261
Async XLA Ops:
  1.3 8.8 %collective-permute-start.1 = (f32[2,64,256]{2,1,0:T(8,128)S(1)}, f32[2,64,256]{2,1,0:T(8,128)S(1)}, u32[]{:S(2)}, u32[]{:S(2)}) collective-permute-start(f32[2,64,256]{2,1,0:T(8,128)S(1)} %get-tuple-element.24), channel_id=1, source_target_pairs={{0,1},{1,0},{2,3},{3,2},{4,5},{5,4},{6,7},{7,6},{8,9},{9,8},{10,11... | collective-permute-start | bytes 393224 | tf_op jit(solution)/shard_map/ppermute | solution.py:337
  4.3 5.8 %collective-permute-start = (f32[8,64,256]{2,1,0:T(8,128)S(1)}, f32[8,64,256]{2,1,0:T(8,128)S(1)}, u32[]{:S(2)}, u32[]{:S(2)}) collective-permute-start(f32[8,64,256]{2,1,0:T(8,128)S(1)} %get-tuple-element.25.dense_ref.refs_2_), channel_id=1, source_target_pairs={{0,8},{8,0},{16,24},{24,16},{1,9},{9,1},{17,25},{25,17},{2,10},{10... | collective-permute-start | bytes 1572872 | tf_op jit(solution)/shard_map/ppermute | solution.py:327
  4.3 15.0 %collective-permute-start.4 = (f32[8,64,256]{2,1,0:T(8,128)S(1)}, f32[8,64,256]{2,1,0:T(8,128)S(1)}, u32[]{:S(2)}, u32[]{:S(2)}) collective-permute-start(f32[8,64,256]{2,1,0:T(8,128)S(1)} %get-tuple-element.25.dense_ref.refs_2_), channel_id=1, source_target_pairs={{0,24},{8,16},{16,8},{24,0},{1,25},{9,17},{17,9},{25,1},{2,26},{10... | collective-permute-start | bytes 1572872 | tf_op jit(solution)/shard_map/ppermute | solution.py:328
  6.0 8.1 %collective-permute-start.2 = (f32[3,64,256]{2,1,0:T(8,128)S(1)}, f32[3,64,256]{2,1,0:T(8,128)S(1)}, u32[]{:S(2)}, u32[]{:S(2)}) collective-permute-start(f32[3,64,256]{2,1,0:T(8,128)S(1)} %get-tuple-element.28), channel_id=1, source_target_pairs={{0,1},{1,0},{2,3},{3,2},{4,5},{5,4},{6,7},{7,6},{8,9},{9,8},{10,11... | collective-permute-start | bytes 589832 | tf_op jit(solution)/shard_map/ppermute | solution.py:337
  6.5 9.2 %collective-permute-start.7 = (f32[3,64,256]{2,1,0:T(8,128)S(1)}, f32[3,64,256]{2,1,0:T(8,128)S(1)}, u32[]{:S(2)}, u32[]{:S(2)}) collective-permute-start(f32[3,64,256]{2,1,0:T(8,128)S(1)} %get-tuple-element.30), channel_id=1, source_target_pairs={{0,6},{1,3},{2,0},{3,5},{4,2},{5,7},{6,4},{7,1},{8,14},{9,11},{10,... | collective-permute-start | bytes 589832 | tf_op jit(solution)/shard_map/ppermute | solution.py:323
  10.1 8.5 %collective-permute-start.3 = (f32[3,64,256]{2,1,0:T(8,128)S(1)}, f32[3,64,256]{2,1,0:T(8,128)S(1)}, u32[]{:S(2)}, u32[]{:S(2)}) collective-permute-start(f32[3,64,256]{2,1,0:T(8,128)S(1)} %get-tuple-element.30), channel_id=1, source_target_pairs={{0,1},{1,0},{2,3},{3,2},{4,5},{5,4},{6,7},{7,6},{8,9},{9,8},{10,11... | collective-permute-start | bytes 589832 | tf_op jit(solution)/shard_map/ppermute | solution.py:337
  10.1 10.3 %collective-permute-start.5 = (f32[2,64,256]{2,1,0:T(8,128)S(1)}, f32[2,64,256]{2,1,0:T(8,128)S(1)}, u32[]{:S(2)}, u32[]{:S(2)}) collective-permute-start(f32[2,64,256]{2,1,0:T(8,128)S(1)} %collective-permute-done.1.refs_3_), channel_id=1, source_target_pairs={{0,2},{1,7},{2,4},{3,1},{4,6},{5,3},{6,0},{7,5},{8,10},{9,15},{10,... | collective-permute-start | bytes 393224 | tf_op jit(solution)/shard_map/ppermute | solution.py:350
  14.0 8.0 %collective-permute-start.6 = (f32[3,64,256]{2,1,0:T(8,128)S(1)}, f32[3,64,256]{2,1,0:T(8,128)S(1)}, u32[]{:S(2)}, u32[]{:S(2)}) collective-permute-start(f32[3,64,256]{2,1,0:T(8,128)S(1)} %collective-permute-done.2.refs_4_), channel_id=1, source_target_pairs={{0,2},{1,7},{2,4},{3,1},{4,6},{5,3},{6,0},{7,5},{8,10},{9,15},{10,... | collective-permute-start | bytes 589832 | tf_op jit(solution)/shard_map/ppermute | solution.py:350
  15.7 6.7 %collective-permute-start.8 = (f32[3,64,256]{2,1,0:T(8,128)S(1)}, f32[3,64,256]{2,1,0:T(8,128)S(1)}, u32[]{:S(2)}, u32[]{:S(2)}) collective-permute-start(f32[3,64,256]{2,1,0:T(8,128)S(1)} %collective-permute-done.7), channel_id=1, source_target_pairs={{0,1},{1,0},{2,3},{3,2},{4,5},{5,4},{6,7},{7,6},{8,9},{9,8},{10,11... | collective-permute-start | bytes 589832 | tf_op jit(solution)/shard_map/ppermute | solution.py:355

commit v2 on v1

--- a/solution.py
+++ b/solution.py
@@ -7,14 +7,12 @@
 from jax.experimental.pallas import tpu as pltpu
 from jax.sharding import PartitionSpec as P
 
-CFG = {'parts': (2, 3, 3), 'x3': 'f', 'lrc': 1, 'la': 0, 'tick': 1, 'ck': 100000000000, 'gk': (0, 2), 'gr': 'tick', 'gf': (1, 2), 'rg': None, 'cut': 8, 'pr': ((0, 1), (3, 4)), 'fo': (0, 1, 2), 'fl': [1], 'cl': 100000000, 'ct': 1000, 'cp': 100000000, 'ca': 1000000000, 'cz': 100000000}
-
 BS = 64
 KA = 7
 KP = 4
 CA = 4
 WIDE = CA * BS
-PARTS = CFG['parts']
+PARTS = (2, 3, 3)
 
 OWN, PAIR_COL, FAR_COL, PAIR_ROW, FAR_ROW = range(5)
 
@@ -128,25 +126,21 @@
     return copy
 
 
-def left_kernel(col_count, first, dense_ref, columns_ref, a_ref, *refs):
-    left, a, columns, sems = refs[-4:]
-    rows = dense_ref.shape[0]
-    mine = a.shape[0]
+def left_kernel(col_count, dense_ref, columns_ref, a_ref, left, a, columns, sems):
+    rows = a_ref.shape[0]
     grid_row = lax.axis_index("row")
     grid_col = lax.axis_index("col")
     small = pltpu.make_async_copy(columns_ref, columns, sems.at[0])
     small.start()
-    large = [pltpu.make_async_copy(a_ref.at[first + row], a.at[row], sems.at[1 + row]) for row in range(mine)]
+    large = [pltpu.make_async_copy(a_ref.at[row], a.at[row], sems.at[1 + row]) for row in range(rows)]
     for copy in large:
         copy.start()
-    if first == 0:
-        left[...] = jnp.zeros_like(left)
+    left[...] = jnp.zeros_like(left)
     for copy in large:
         copy.wait()
     small.wait()
-    for index in range(mine):
-        row = first + index
-        a_high, a_low = split(a[index])
+    for row in range(rows):
+        a_high, a_low = split(a[row])
         p_high, p_low = split(dense_ref[row])
         turned_a = jnp.concatenate([a_high, a_low], axis=0).T
         term = jnp.dot(
@@ -166,24 +160,22 @@
             left[pl.ds(at, BS), :] += term[slot * BS : (slot + 1) * BS]
 
 
-def left_product(dense, a_columns, a_values, before, first, count, col_count):
+def left_product(dense, a_columns, a_values, col_count):
     rows = a_values.shape[0]
-    given = [] if before is None else [before]
     return pl.pallas_call(
-        functools.partial(left_kernel, col_count, first),
-        in_specs=[VMEM, HBM, HBM] + [VMEM] * len(given),
+        functools.partial(left_kernel, col_count),
+        in_specs=[VMEM, HBM, HBM],
         out_specs=VMEM,
         out_shape=pltpu.VMEM((5 * rows * BS, WIDE), jnp.float32),
         scratch_shapes=[
-            pltpu.VMEM((count, *a_values.shape[1:]), jnp.float32),
+            pltpu.VMEM(a_values.shape, jnp.float32),
             pltpu.SMEM(a_columns.shape, jnp.int32),
-            pltpu.SemaphoreType.DMA((1 + count,)),
+            pltpu.SemaphoreType.DMA((1 + rows,)),
         ],
-        input_output_aliases={3: 0} if given else {},
         compiler_params=pltpu.CompilerParams(vmem_limit_bytes=16 * MIB),
-        cost_estimate=cost(CFG['cl'], 4000),
+        cost_estimate=cost(100000000, 4000),
         name="left_product",
-    )(in_vmem(dense), in_hbm(a_columns), in_hbm(a_values), *map(in_vmem, given))
+    )(in_vmem(dense), in_hbm(a_columns), in_hbm(a_values))
 
 
 def turn_kernel(left_ref, high_ref, low_ref):
@@ -200,7 +192,7 @@
         out_specs=[VMEM, VMEM],
         out_shape=[pltpu.VMEM((5, WIDE, depth), jnp.bfloat16)] * 2,
         compiler_params=pltpu.CompilerParams(vmem_limit_bytes=16 * MIB),
-        cost_estimate=cost(CFG['ct'], 5000),
+        cost_estimate=cost(1000, 5000),
         name="turned",
     )(in_vmem(left))
 
@@ -267,7 +259,7 @@
         input_output_aliases={0: 0} if given_out else {},
         compiler_params=pltpu.CompilerParams(vmem_limit_bytes=16 * MIB),
         cost_estimate=cost(flops, 2000),
-        name="last_product" if final else "stage%d%sf%d" % (len(sums), "p" if plan[0][0] == FAR_COL else "", len(flush)),
+        name="last_stage" if final else "stage",
     )(*given_out, *map(in_vmem, (high, low, *flat)))
     if writes:
         out, *totals = totals
@@ -298,78 +290,45 @@
     return lax.optimization_barrier((value, *others))[0]
 
 
-def tick_kernel(value_ref, out_ref):
+def mark_kernel(value_ref, out_ref):
     out_ref[...] = value_ref[0, :8, :128]
 
 
-def tick(value, flops):
+def mark(value, flops):
     return pl.pallas_call(
-        tick_kernel,
+        mark_kernel,
         in_specs=[VMEM],
         out_specs=VMEM,
         out_shape=pltpu.VMEM((8, 128), jnp.float32),
         cost_estimate=cost(flops, 2000),
-        name="tick",
+        name="mark",
     )(in_vmem(value))
 
 
 def per_device(a_values, a_columns, p_values, p_columns, p_count, aggregates):
     row_count = lax.axis_size("row")
     col_count = lax.axis_size("col")
-    rows = a_values.shape[0]
     pairs, onward = column_pairs(col_count), column_onward(col_count)
     parts, dense = dense_rows(p_values, p_columns, p_count, aggregates)
-    ticked = tick(parts[0], CFG['ck']) if CFG['tick'] else None
+    started = mark(parts[0], 100000000000)
     direct = lax.ppermute(parts[-1], "col", two_on(col_count))
-    to_row = dense
-    if CFG['rg'] == 'tick' and CFG['tick']:
-        to_row = after(dense, ticked)
     pair_row = lax.ppermute(dense, "row", row_pairs(row_count))
-    far_row = lax.ppermute(to_row, "row", beyond(row_count))
-    pair = []
-    for index, part in enumerate(parts):
-        if index == len(parts) - 1 and CFG['x3'] == 'f':
-            part = after(part, pair[0])
-        elif index == len(parts) - 1 and CFG['x3'] == 'd':
-            part = after(part, direct)
-        elif index == len(parts) - 1 and CFG['x3'] == 'r':
-            part = after(part, pair_row)
-        pair.append(lax.ppermute(part, "col", pairs))
-    own = dense
-    if CFG['lrc']:
-        own = after(own, pair_row)
-    if CFG['la'] is not None:
-        own = after(own, pair[CFG['la']])
-    left = left_product(own, a_columns, a_values, None, 0, rows, col_count)
-    far = []
-    for index, part in enumerate(pair[:-1]):
-        if index in CFG['gf']:
-            part = after(part, left)
-        if CFG['tick'] and index in CFG['gk']:
-            part = after(part, ticked)
-        far.append(lax.ppermute(part, "col", onward))
-    if CFG['gr'] == 'left':
-        direct = after(direct, left)
-    elif CFG['gr'] == 'tick' and CFG['tick']:
-        direct = after(direct, ticked)
-    far.append(lax.ppermute(direct, "col", pairs))
+    far_row = lax.ppermute(dense, "row", beyond(row_count))
+    pair = [lax.ppermute(part, "col", pairs) for part in parts[:-1]]
+    pair.append(lax.ppermute(after(parts[-1], pair[0]), "col", pairs))
+    left = left_product(after(after(dense, pair_row), pair[0]), a_columns, a_values, col_count)
+    far = [lax.ppermute(after(pair[0], started), "col", onward)]
+    far.append(lax.ppermute(after(pair[1], left), "col", onward))
+    far.append(lax.ppermute(after(direct, started), "col", pairs))
     high, low = turned(left)
-    given = {OWN: [dense], PAIR_ROW: [pair_row], FAR_ROW: [far_row], PAIR_COL: pair}
-    ats = [sum(PARTS[:k]) * BS for k in range(len(PARTS))]
-    steps = [{place: (given[place], 0) for place in group} for group in CFG['pr']]
-    steps += [{FAR_COL: ([far[k]], ats[k])} for k in CFG['fo']]
-    out, ready, before = None, {}, None
-    for step, what in enumerate(steps):
-        last = step == len(steps) - 1
-        now = step in CFG['fl'] or last
-        sums = {place: (*some, before if place == FAR_COL else None) for place, some in what.items()}
-        flops = CFG['cz'] if last else CFG['ca'] if FAR_COL in what else CFG['cp']
-        out, totals = stage(out, high, low, ready if now else {}, sums, flops, last)
-        ready = {} if now else ready
-        if not last:
-            before = totals.pop(FAR_COL, before)
-            ready = {**ready, **totals}
-    return out
+    places = {OWN: [dense], PAIR_COL: pair}, {PAIR_ROW: [pair_row], FAR_ROW: [far_row]}
+    _, ready = stage(None, high, low, {}, {place: (whole, 0, None) for place, whole in places[0].items()}, 100000000)
+    out, blocks = stage(None, high, low, ready, {place: (whole, 0, None) for place, whole in places[1].items()}, 100000000)
+    at, before = 0, None
+    for part in far[:-1]:
+        _, totals = stage(None, high, low, {}, {FAR_COL: ([part], at, before)}, 1000000000)
+        at, before = at + part.shape[0] * BS, totals[FAR_COL]
+    return stage(out, high, low, blocks, {FAR_COL: ([far[-1]], at, before)}, 100000000, True)[0]
 
 
 def solution(mesh):

time: 23.6 us -> 23.6 us (level)
  no operation moved by 1% of the time
where the time goes in v2:
time: 23.6 us; the launch traced here: 23.4 us
  starting transfers between devices  14.1 us (60%)
  Pallas kernels  7.85 us (33%)
  waiting for transfers between devices  1.37 us (6%)
    ppermute x1, starting transfers between devices, per_device(): direct = lax.ppermute(parts[-1], 'col', two_on(col_count))  3.6 us
    ppermute x2, starting transfers between devices, per_device(): pair = [lax.ppermute(part, 'col', pairs) for part in parts[:-1]]  3.54 us
    pallas_call x5, Pallas kernels, stage(): pl.pallas_call(functools.partial(stage_kernel, bool(given_out), tuple(flu...  3.37 us
    pallas_call x1, Pallas kernels, left_product(): pl.pallas_call(functools.partial(left_kernel, col_count), in_specs=[VMEM,...  2.43 us
    ppermute x1, starting transfers between devices, per_device(): far.append(lax.ppermute(after(direct, started), 'col', pairs))  2.2 us
    ppermute x1, starting transfers between devices, per_device(): far_row = lax.ppermute(dense, 'row', beyond(row_count))  1.63 us
    ppermute x1, starting transfers between devices, per_device(): far.append(lax.ppermute(after(pair[1], left), 'col', onward))  1.63 us
    ppermute x1, starting transfers between devices, per_device(): far = [lax.ppermute(after(pair[0], started), 'col', onward)]  1.47 us
  transfers between devices with their start and end apart: 9, of which 1 were waited for; matrix products, arithmetic and copies ran while one was open for 0% of the time, Pallas kernels for 23%

profile of v2, /device:TPU:0, one launch (start us, length us, event | category | flops | bytes accessed | tf_op | source)
XLA Modules:
  0.0 23.4 jit_solution(214512686551528442)
XLA Ops:
  0.0 1.3 %dense_rows.1 = (f32[2,64,256]{2,1,0:T(8,128)S(1)}, f32[3,64,256]{2,1,0:T(8,128)S(1)}, f32[3,64,256]{2,1,0:T(8,128)S(1)}, f32[8,64,256]{2,1,0:T(8,128)S(1)}) custom-call(f32[8,64,256]{2,1,0:T(8,128)} %values_ref.1, s32[4,8]{1,0:T(4,128)} %bitcast.1, s32[8]{0:T(128)} %counts_ref.1, s32[8]{0:T(128)} %aggregates_ref.1), custom_call_target="tpu_custom_call" | custom-call | flops 400000 | bytes 1572864 | tf_op jit(solution)/shard_map/dense_rows/pallas_call | solution.py:104
  1.3 3.0 %collective-permute-start.1 = (f32[2,64,256]{2,1,0:T(8,128)S(1)}, f32[2,64,256]{2,1,0:T(8,128)S(1)}, u32[]{:S(2)}, u32[]{:S(2)}) collective-permute-start(f32[2,64,256]{2,1,0:T(8,128)S(1)} %get-tuple-element.24), channel_id=1, source_target_pairs={{0,1},{1,0},{2,3},{3,2},{4,5},{5,4},{6,7},{7,6},{8,9},{9,8},{10,11... | collective-permute-start | bytes 393224 | tf_op jit(solution)/shard_map/ppermute | solution.py:317
  4.3 0.0 collective-permute-start
  4.3 1.6 %collective-permute-start.4 = (f32[8,64,256]{2,1,0:T(8,128)S(1)}, f32[8,64,256]{2,1,0:T(8,128)S(1)}, u32[]{:S(2)}, u32[]{:S(2)}) collective-permute-start(f32[8,64,256]{2,1,0:T(8,128)S(1)} %get-tuple-element.25.dense_ref.refs_2_), channel_id=1, source_target_pairs={{0,24},{8,16},{16,8},{24,0},{1,25},{9,17},{17,9},{25,1},{2,26},{10... | collective-permute-start | bytes 1572872 | tf_op jit(solution)/shard_map/ppermute | solution.py:316
  6.0 0.5 %collective-permute-start.2 = (f32[3,64,256]{2,1,0:T(8,128)S(1)}, f32[3,64,256]{2,1,0:T(8,128)S(1)}, u32[]{:S(2)}, u32[]{:S(2)}) collective-permute-start(f32[3,64,256]{2,1,0:T(8,128)S(1)} %get-tuple-element.28), channel_id=1, source_target_pairs={{0,1},{1,0},{2,3},{3,2},{4,5},{5,4},{6,7},{7,6},{8,9},{9,8},{10,11... | collective-permute-start | bytes 589832 | tf_op jit(solution)/shard_map/ppermute | solution.py:317
  6.5 3.6 %collective-permute-start.7 = (f32[3,64,256]{2,1,0:T(8,128)S(1)}, f32[3,64,256]{2,1,0:T(8,128)S(1)}, u32[]{:S(2)}, u32[]{:S(2)}) collective-permute-start(f32[3,64,256]{2,1,0:T(8,128)S(1)} %get-tuple-element.30), channel_id=1, source_target_pairs={{0,6},{1,3},{2,0},{3,5},{4,2},{5,7},{6,4},{7,1},{8,14},{9,11},{10,... | collective-permute-start | bytes 589832 | tf_op jit(solution)/shard_map/ppermute | solution.py:314
  10.1 0.0 collective-permute-done.1.refs_3_
  10.1 0.0 collective-permute-start.3
  10.1 0.0 collective-permute-done.refs_4_
  10.1 1.5 %collective-permute-start.5 = (f32[2,64,256]{2,1,0:T(8,128)S(1)}, f32[2,64,256]{2,1,0:T(8,128)S(1)}, u32[]{:S(2)}, u32[]{:S(2)}) collective-permute-start(f32[2,64,256]{2,1,0:T(8,128)S(1)} %collective-permute-done.1.refs_3_), channel_id=1, source_target_pairs={{0,2},{1,7},{2,4},{3,1},{4,6},{5,3},{6,0},{7,5},{8,10},{9,15},{10,... | collective-permute-start | bytes 393224 | tf_op jit(solution)/shard_map/ppermute | solution.py:320
  11.6 2.4 %left_product.1.left_ref = f32[2560,256]{1,0:T(8,128)S(1)} custom-call(f32[8,64,256]{2,1,0:T(8,128)S(1)} %get-tuple-element.25.dense_ref.refs_2_, s32[8,7]{1,0:T(8,128)} %columns_ref.1, f32[8,64,448]{2,1,0:T(8,128)} %a_ref.1), custom_call_target="tpu_custom_call" | custom-call | flops 100000000 | bytes 4000 | tf_op jit(solution)/shard_map/left_product/pallas_call | solution.py:165
  14.0 0.0 collective-permute-done.2.refs_4_
  14.0 1.6 %collective-permute-start.6 = (f32[3,64,256]{2,1,0:T(8,128)S(1)}, f32[3,64,256]{2,1,0:T(8,128)S(1)}, u32[]{:S(2)}, u32[]{:S(2)}) collective-permute-start(f32[3,64,256]{2,1,0:T(8,128)S(1)} %collective-permute-done.2.refs_4_), channel_id=1, source_target_pairs={{0,2},{1,7},{2,4},{3,1},{4,6},{5,3},{6,0},{7,5},{8,10},{9,15},{10,... | collective-permute-start | bytes 589832 | tf_op jit(solution)/shard_map/ppermute | solution.py:321
  15.7 0.0 collective-permute-done.7
  15.7 2.2 %collective-permute-start.8 = (f32[3,64,256]{2,1,0:T(8,128)S(1)}, f32[3,64,256]{2,1,0:T(8,128)S(1)}, u32[]{:S(2)}, u32[]{:S(2)}) collective-permute-start(f32[3,64,256]{2,1,0:T(8,128)S(1)} %collective-permute-done.7), channel_id=1, source_target_pairs={{0,1},{1,0},{2,3},{3,2},{4,5},{5,4},{6,7},{7,6},{8,9},{9,8},{10,11... | collective-permute-start | bytes 589832 | tf_op jit(solution)/shard_map/ppermute | solution.py:322
  17.9 0.7 %turned.1 = (bf16[5,256,512]{2,1,0:T(8,128)(2,1)S(1)}, bf16[5,256,512]{2,1,0:T(8,128)(2,1)S(1)}) custom-call(f32[2560,256]{1,0:T(8,128)S(1)} %left_product.1.left_ref), custom_call_target="tpu_custom_call" | custom-call | flops 1000 | bytes 5000 | tf_op jit(solution)/shard_map/turned/pallas_call | solution.py:189
  18.6 0.0 collective-permute-done.3.refs_5_
  18.6 0.7 %stage.4 = (f32[4,64,256]{2,1,0:T(8,128)S(1)}, f32[4,64,256]{2,1,0:T(8,128)S(1)}) custom-call(bf16[5,256,512]{2,1,0:T(8,128)(2,1)S(1)} %get-tuple-element.26.refs_0_.refs_1_, bf16[5,256,512]{2,1,0:T(8,128)(2,1)S(1)} %get-tuple-element.27.refs_1_.refs_2_, f32[8,64,256]{2,1,0:T(8,128)S(1)} %get-tuple-element.25.dense_ref.refs_2_, ...), custom_call_target="tpu_custom_call" | custom-call | flops 100000000 | bytes 2000 | tf_op jit(solution)/shard_map/stage/pallas_call | solution.py:253
  19.3 0.0 collective-permute-done.4.refs_5_
  19.3 1.1 %stage.5 = (f32[4,64,1280]{2,1,0:T(8,128)}, f32[4,64,256]{2,1,0:T(8,128)S(1)}, f32[4,64,256]{2,1,0:T(8,128)S(1)}) custom-call(bf16[5,256,512]{2,1,0:T(8,128)(2,1)S(1)} %get-tuple-element.26.refs_0_.refs_1_, bf16[5,256,512]{2,1,0:T(8,128)(2,1)S(1)} %get-tuple-element.27.refs_1_.refs_2_, f32[4,64,256]{2,1,0:T(8,128)S(1)} %get-tuple-element.31.refs_2_, ...), custom_call_target="tpu_custom_call" | custom-call | flops 100000000 | bytes 2000 | tf_op jit(solution)/shard_map/stage/pallas_call | solution.py:253
  20.4 0.0 collective-permute-done.5.refs_2_
  20.4 0.3 %stage.6.refs_2_ = f32[4,64,256]{2,1,0:T(8,128)S(1)} custom-call(bf16[5,256,512]{2,1,0:T(8,128)(2,1)S(1)} %get-tuple-element.26.refs_0_.refs_1_, bf16[5,256,512]{2,1,0:T(8,128)(2,1)S(1)} %get-tuple-element.27.refs_1_.refs_2_, f32[2,64,256]{2,1,0:T(8,128)S(1)} %collective-permute-done.5.refs_2_), custom_call_target="tpu_custom_call" | custom-call | flops 1000000000 | bytes 2000 | tf_op jit(solution)/shard_map/stage/pallas_call | solution.py:253
  20.7 1.3 %collective-permute-done.6.refs_3_ = f32[3,64,256]{2,1,0:T(8,128)S(1)} collective-permute-done((f32[3,64,256]{2,1,0:T(8,128)S(1)}, f32[3,64,256]{2,1,0:T(8,128)S(1)}, u32[]{:S(2)}, u32[]{:S(2)}) %collective-permute-start.6) | collective-permute-done | bytes 196640 | tf_op jit(solution)/shard_map/ppermute | solution.py:321
  22.1 0.3 %stage.7.refs_5_ = f32[4,64,256]{2,1,0:T(8,128)S(1)} custom-call(bf16[5,256,512]{2,1,0:T(8,128)(2,1)S(1)} %get-tuple-element.26.refs_0_.refs_1_, bf16[5,256,512]{2,1,0:T(8,128)(2,1)S(1)} %get-tuple-element.27.refs_1_.refs_2_, f32[4,64,256]{2,1,0:T(8,128)S(1)} %stage.6.refs_2_, f32[3,64,256]{2,1,0:T(8,128)S(1)} %collective-permute-done.6.refs_3_), custom_call_target="tpu_custom_call" | custom-call | flops 1000000000 | bytes 2000 | tf_op jit(solution)/shard_map/stage/pallas_call | solution.py:253
  22.4 0.0 collective-permute-done.8.refs_6_
  22.4 1.0 %last_stage.1 = f32[4,64,1280]{2,1,0:T(8,128)} custom-call(f32[4,64,1280]{2,1,0:T(8,128)} %get-tuple-element.33.refs_0_, bf16[5,256,512]{2,1,0:T(8,128)(2,1)S(1)} %get-tuple-element.26.refs_0_.refs_1_, bf16[5,256,512]{2,1,0:T(8,128)(2,1)S(1)} %get-tuple-element.27.refs_1_.refs_2_, ...), custom_call_target="tpu_custom_call", output_to_operand_aliasing={{}: (0, {})} | custom-call | flops 100000000 | bytes 2000 | tf_op jit(solution)/shard_map/last_stage/pallas_call | solution.py:253
Async XLA Ops:
  1.3 8.8 %collective-permute-start.1 = (f32[2,64,256]{2,1,0:T(8,128)S(1)}, f32[2,64,256]{2,1,0:T(8,128)S(1)}, u32[]{:S(2)}, u32[]{:S(2)}) collective-permute-start(f32[2,64,256]{2,1,0:T(8,128)S(1)} %get-tuple-element.24), channel_id=1, source_target_pairs={{0,1},{1,0},{2,3},{3,2},{4,5},{5,4},{6,7},{7,6},{8,9},{9,8},{10,11... | collective-permute-start | bytes 393224 | tf_op jit(solution)/shard_map/ppermute | solution.py:317
  4.3 5.8 %collective-permute-start = (f32[8,64,256]{2,1,0:T(8,128)S(1)}, f32[8,64,256]{2,1,0:T(8,128)S(1)}, u32[]{:S(2)}, u32[]{:S(2)}) collective-permute-start(f32[8,64,256]{2,1,0:T(8,128)S(1)} %get-tuple-element.25.dense_ref.refs_2_), channel_id=1, source_target_pairs={{0,8},{8,0},{16,24},{24,16},{1,9},{9,1},{17,25},{25,17},{2,10},{10... | collective-permute-start | bytes 1572872 | tf_op jit(solution)/shard_map/ppermute | solution.py:315
  4.3 15.0 %collective-permute-start.4 = (f32[8,64,256]{2,1,0:T(8,128)S(1)}, f32[8,64,256]{2,1,0:T(8,128)S(1)}, u32[]{:S(2)}, u32[]{:S(2)}) collective-permute-start(f32[8,64,256]{2,1,0:T(8,128)S(1)} %get-tuple-element.25.dense_ref.refs_2_), channel_id=1, source_target_pairs={{0,24},{8,16},{16,8},{24,0},{1,25},{9,17},{17,9},{25,1},{2,26},{10... | collective-permute-start | bytes 1572872 | tf_op jit(solution)/shard_map/ppermute | solution.py:316
  6.0 8.1 %collective-permute-start.2 = (f32[3,64,256]{2,1,0:T(8,128)S(1)}, f32[3,64,256]{2,1,0:T(8,128)S(1)}, u32[]{:S(2)}, u32[]{:S(2)}) collective-permute-start(f32[3,64,256]{2,1,0:T(8,128)S(1)} %get-tuple-element.28), channel_id=1, source_target_pairs={{0,1},{1,0},{2,3},{3,2},{4,5},{5,4},{6,7},{7,6},{8,9},{9,8},{10,11... | collective-permute-start | bytes 589832 | tf_op jit(solution)/shard_map/ppermute | solution.py:317
  6.5 9.2 %collective-permute-start.7 = (f32[3,64,256]{2,1,0:T(8,128)S(1)}, f32[3,64,256]{2,1,0:T(8,128)S(1)}, u32[]{:S(2)}, u32[]{:S(2)}) collective-permute-start(f32[3,64,256]{2,1,0:T(8,128)S(1)} %get-tuple-element.30), channel_id=1, source_target_pairs={{0,6},{1,3},{2,0},{3,5},{4,2},{5,7},{6,4},{7,1},{8,14},{9,11},{10,... | collective-permute-start | bytes 589832 | tf_op jit(solution)/shard_map/ppermute | solution.py:314
  10.1 8.5 %collective-permute-start.3 = (f32[3,64,256]{2,1,0:T(8,128)S(1)}, f32[3,64,256]{2,1,0:T(8,128)S(1)}, u32[]{:S(2)}, u32[]{:S(2)}) collective-permute-start(f32[3,64,256]{2,1,0:T(8,128)S(1)} %get-tuple-element.30), channel_id=1, source_target_pairs={{0,1},{1,0},{2,3},{3,2},{4,5},{5,4},{6,7},{7,6},{8,9},{9,8},{10,11... | collective-permute-start | bytes 589832 | tf_op jit(solution)/shard_map/ppermute | solution.py:318
  10.1 10.3 %collective-permute-start.5 = (f32[2,64,256]{2,1,0:T(8,128)S(1)}, f32[2,64,256]{2,1,0:T(8,128)S(1)}, u32[]{:S(2)}, u32[]{:S(2)}) collective-permute-start(f32[2,64,256]{2,1,0:T(8,128)S(1)} %collective-permute-done.1.refs_3_), channel_id=1, source_target_pairs={{0,2},{1,7},{2,4},{3,1},{4,6},{5,3},{6,0},{7,5},{8,10},{9,15},{10,... | collective-permute-start | bytes 393224 | tf_op jit(solution)/shard_map/ppermute | solution.py:320
  14.0 8.0 %collective-permute-start.6 = (f32[3,64,256]{2,1,0:T(8,128)S(1)}, f32[3,64,256]{2,1,0:T(8,128)S(1)}, u32[]{:S(2)}, u32[]{:S(2)}) collective-permute-start(f32[3,64,256]{2,1,0:T(8,128)S(1)} %collective-permute-done.2.refs_4_), channel_id=1, source_target_pairs={{0,2},{1,7},{2,4},{3,1},{4,6},{5,3},{6,0},{7,5},{8,10},{9,15},{10,... | collective-permute-start | bytes 589832 | tf_op jit(solution)/shard_map/ppermute | solution.py:321
  15.7 6.7 %collective-permute-start.8 = (f32[3,64,256]{2,1,0:T(8,128)S(1)}, f32[3,64,256]{2,1,0:T(8,128)S(1)}, u32[]{:S(2)}, u32[]{:S(2)}) collective-permute-start(f32[3,64,256]{2,1,0:T(8,128)S(1)} %collective-permute-done.7), channel_id=1, source_target_pairs={{0,1},{1,0},{2,3},{3,2},{4,5},{5,4},{6,7},{7,6},{8,9},{9,8},{10,11... | collective-permute-start | bytes 589832 | tf_op jit(solution)/shard_map/ppermute | solution.py:322
